TPU v7x, 512 devices: a whole 4x4x16 slice. The times are simulated.
512 devices in a mesh: space: 32 (over z, core), mode: 16 (over y, x).
Axes of the slice: x: 4, y: 4, z: 16, core: 2. Of those that a mesh axis runs over, the one named last changes fastest.
Arguments:
- basis: float32 [3, 256, 16, 8, 2048], P(None, 'space', None, None, 'mode'), may hold values from -132 to 132
- mean_flow: float32 [3, 256, 16, 8], P(None, 'space'), may hold values from -3 to 3
- flow_gradient: float32 [3, 3, 256, 16, 8], P(None, None, 'space'), may hold values from -2 to 2
- viscosity: float32 [256, 16, 8], P('space'), may hold values from 0.02 to 0.2
Outputs:
- reduced: float32 [2048, 2048], P('mode', 'space')
- advected: float32 [3, 256, 16, 8, 2048], P(None, 'space', None, None, 'mode')
- r_factor: float32 [2048, 128], P('mode')
All inputs are finite; a program needn't handle non-finite values.
Results may differ from a plain program's by a relative error of at most 0.00074.
Values may be sent and summed in bfloat16 or wider, within the bound.
No kernel may reach another device: no remote copies, remote signals or barrier semaphores. Data moves between devices by JAX's collectives and lax.ppermute only.
A program may use at most 64 MiB of HBM per device.

v0:
```python
import jax
import jax.numpy as jnp
from jax import lax
from jax.sharding import PartitionSpec as P


def extended(cells, sides, width):
    for axis, dim in sides:
        count = lax.axis_size(axis)
        ends = count - 1
        head = lax.slice_in_dim(cells, 0, width, axis=dim)
        tail = lax.slice_in_dim(cells, cells.shape[dim] - width, cells.shape[dim], axis=dim)
        cells = jnp.concatenate(
            [
                lax.ppermute(tail, axis, [(i, (i + 1) % count) for i in range(ends)]),
                cells,
                lax.ppermute(head, axis, [((i + 1) % count, i) for i in range(ends)]),
            ],
            axis=dim,
        )
    return cells


def transport(padded, mean_flow, flow_gradient, viscosity):
    center = padded[:, 1:-1]
    widen_y = jnp.pad(center, ((0, 0), (0, 0), (1, 1), (0, 0), (0, 0)))
    widen_z = jnp.pad(center, ((0, 0), (0, 0), (0, 0), (1, 1), (0, 0)))
    east_side = padded[:, 2:]
    west_side = padded[:, :-2]
    north_side = widen_y[:, :, 2:]
    south_side = widen_y[:, :, :-2]
    upper_side = widen_z[:, :, :, 2:]
    lower_side = widen_z[:, :, :, :-2]
    laplacian = (
        east_side + west_side + north_side + south_side + upper_side + lower_side - 6.0 * center
    )
    advection = 0.5 * (
        mean_flow[0][None, :, :, :, None] * (east_side - west_side)
        + mean_flow[1][None, :, :, :, None] * (north_side - south_side)
        + mean_flow[2][None, :, :, :, None] * (upper_side - lower_side)
    )
    coupling = flow_gradient[:, 0][..., None] * center[0][None]
    coupling = coupling + flow_gradient[:, 1][..., None] * center[1][None]
    coupling = coupling + flow_gradient[:, 2][..., None] * center[2][None]
    return viscosity[None, :, :, :, None] * laplacian - advection - coupling


def apply_inverse(field, lower_factor):
    width = field.shape[4]
    flat_rows = field.reshape(-1, width)
    solved = jax.scipy.linalg.solve_triangular(lower_factor, flat_rows.T, lower=True)
    return solved.T.reshape(field.shape)


def body(basis, mean_flow, flow_gradient, viscosity):
    cells_x = basis.shape[1]
    cells_y = basis.shape[2]
    cells_z = basis.shape[3]
    panel_width = basis.shape[4]
    weight = 1.0 / (3 * cells_x * cells_y * cells_z * lax.axis_size("space"))
    flat_basis = basis.reshape(-1, panel_width)
    gram_local = (
        jnp.dot(
            flat_basis.T,
            flat_basis,
            precision=lax.Precision.HIGHEST,
            preferred_element_type=jnp.float32,
        )
        * weight
    )
    gram = lax.psum(gram_local, "space")
    lower_factor = jnp.linalg.cholesky(gram)
    ortho = apply_inverse(basis, lower_factor)
    padded_ortho = extended(ortho, (("space", 1),), 1)
    advected = transport(padded_ortho, mean_flow, flow_gradient, viscosity)
    rounded_images = advected.astype(jnp.bfloat16)
    rounded_rows = ortho.astype(jnp.bfloat16).reshape(-1, panel_width)
    panel_piece = lax.all_gather(rounded_images, "mode", axis=4, tiled=True)
    piece_rows = panel_piece.reshape(-1, panel_piece.shape[4])
    strip = (
        jnp.einsum("ra,rk->ak", rounded_rows, piece_rows, preferred_element_type=jnp.float32)
        * weight
    )
    reduced = lax.psum_scatter(strip, "space", scatter_dimension=1, tiled=True)
    return (reduced, advected, lower_factor.T)


def solution(mesh):
    placed = (
        P(None, "space", None, None, "mode"),
        P(None, "space", None, None),
        P(None, None, "space", None, None),
        P("space", None, None),
    )
    return jax.shard_map(
        body,
        mesh=mesh,
        in_specs=placed,
        out_specs=(P("mode", "space"), P(None, "space", None, None, "mode"), P("mode", None)),
        check_vma=False,
    )
```

profile of v0, /device:TPU:2, one launch (start us, length us, event | category | flops | bytes accessed | tf_op | source)
XLA Modules:
  0.0 491.2 jit_solution(15039007794072252386)
XLA Ops:
  7.2 0.0 all-reduce.4.cloned.1.call-start
  7.2 1.3 copy-done
  8.6 3.3 fusion.8
  11.9 0.0 all-gather.2.cloned.1.call-start
  12.0 0.6 slice_bitcast_fusion.5
  12.6 186.8 %all-reduce.4.cloned.1.call-done = f32[128,128]{0,1:T(8,128)} async-done(((f32[128,128]{0,1:T(8,128)}), f32[128,128]{0,1:T(8,128)}) %all-reduce.4.cloned.1.call-update) | async-done | bytes 65552 | tf_op jit(solution)/shard_map/psum | solution.py:71
  199.4 0.9 copy.27
  200.3 0.9 fusion.11
  201.2 11.7 %cholesky.16 = f32[128,128]{1,0:T(8,128)S(1)} custom-call(f32[128,128]{1,0:T(8,128)S(1)} %fusion.11), custom_call_target="Cholesky" | custom-call | tf_op jit(solution)/shard_map/jit(cholesky)/cholesky | solution.py:72
  212.9 0.6 compare_reduce_fusion
  213.5 0.7 fusion.12
  214.2 10.4 %custom-call.7 = f32[1,128,128]{1,2,0:T(8,128)} custom-call(f32[1,128,128]{2,1,0:T(8,128)S(1)} %get-tuple-element.23), custom_call_target="InvertDiagBlocksLowerTriangular" | custom-call | tf_op jit(solution)/shard_map/jit(_solve_triangular)/triangular_solve | solution.py:51
  224.7 2.3 convolution_bitcast_fusion
  227.0 1.6 copy.28
  228.6 1.7 copy.30
  230.3 0.8 fusion.14
  231.1 1.3 collective-permute-start
  232.4 3.7 collective-permute-start.1
  236.1 1.2 fusion.15
  237.3 1.3 copy.36
  238.6 0.9 copy.37
  239.5 1.0 copy.40
  240.5 2.1 copy.41
  242.6 2.1 copy.38
  244.7 1.1 copy.39
  245.8 4.9 %fusion.13 = (bf16[3,8,16,8,128]{4,2,3,1,0:T(8,128)(2,1)}, f32[3,8,16,8,128]{4,2,3,1,0:T(8,128)}) fusion(f32[8,16,8,128]{3,1,2,0:T(8,128)} %copy.41, f32[3,8,16,8]{2,3,1,0:T(8,128)S(1)} %get-tuple-element.17, f32[8,16,8,128]{3,1,2,0:T(8,128)S(1)} %copy.39, f32[3,8,16,8]{2,3,1,0:T(8,128)S(1)} %get-tuple-element.18, f32[8,16,8,128]{3,1,2,0:T(8,128)} %copy.37, ...), kind=kLoop, calls=%fused_computation.31 | loop fusion | flops 10616832 | bytes 5951488 | tf_op jit(solution)/shard_map/convert_element_type | solution.py:76
  250.8 0.0 reduce-scatter.2.cloned.1.call-start
  250.9 110.3 %all-gather.2.cloned.1.call-done = bf16[3,8,16,8,2048]{4,2,3,1,0:T(8,128)(2,1)} async-done(((bf16[3,8,16,8,128]{4,2,3,1,0:T(8,128)(2,1)}), bf16[3,8,16,8,2048]{4,2,3,1,0:T(8,128)(2,1)}) %all-gather.2.cloned.1.call-update) | async-done | bytes 12582928 | tf_op jit(solution)/shard_map/all_gather | solution.py:78
  361.1 15.4 %fusion.5 = f32[128,2048]{0,1:T(8,128)} fusion(bf16[3,8,16,8,2048]{4,2,3,1,0:T(8,128)(2,1)} %all-gather.2.cloned.1.call-done, f32[3,8,16,8,128]{4,3,2,1,0:T(8,128)} %bitcast.45), kind=kOutput, calls=%fused_computation.6 | convolution fusion | flops 1611268096 | bytes 15204352 | tf_op jit(solution)/shard_map/ra,rk->ak/dot_general | solution.py:81
  376.6 0.7 copy.44
  377.3 1.7 copy.43
  379.1 105.6 %reduce-scatter.2.cloned.1.call-done = f32[128,64]{0,1:T(8,128)} async-done(((f32[128,2048]{0,1:T(8,128)}), f32[128,64]{0,1:T(8,128)}) %reduce-scatter.2.cloned.1.call-update) | async-done | bytes 32784 | tf_op jit(solution)/shard_map/reduce_scatter | solution.py:84
  (20 shorter events, 0.1 us)
Async XLA Ops:
  7.2 1.4 copy-start
  7.2 4.7 copy-start.5
  7.2 4.8 copy-start.6
  7.2 192.2 %all-reduce.4.cloned.1.call-start = ((), (), s32[]{:S(2)}) async-start(), calls=%async_computation.1 | async-start | bytes 131072 | tf_op jit(solution)/shard_map/psum | solution.py:71
  11.9 349.3 %all-gather.2.cloned.1.call-start = ((), (), s32[]{:S(2)}) async-start(), calls=%async_computation.2 | async-start | bytes 13369344 | tf_op jit(solution)/shard_map/all_gather | solution.py:78
  230.3 7.0 %copy-start.1 = (f32[3,8,16,8,128]{4,2,3,1,0:T(8,128)}, f32[3,8,16,8,128]{4,2,3,1,0:T(8,128)S(1)}, u32[]{:S(2)}) copy-start(f32[3,8,16,8,128]{4,2,3,1,0:T(8,128)S(1)} %copy.30) | copy-start | bytes 4718596
  231.1 14.7 %collective-permute-start = (f32[3,1,16,8,128]{4,2,3,1,0:T(8,128)}, f32[3,1,16,8,128]{4,2,3,1,0:T(8,128)}, u32[]{:S(2)}, u32[]{:S(2)}) collective-permute-start(f32[3,1,16,8,128]{4,2,3,1,0:T(8,128)} %get-tuple-element.11), channel_id=1, source_target_pairs={{16,0},{32,16},{48,32},{64,48},{80,64},{96,80},{112,96},{128,112},... | collective-permute-start | bytes 589832 | tf_op jit(solution)/shard_map/ppermute | solution.py:17
  232.4 13.4 %collective-permute-start.1 = (f32[3,1,16,8,128]{4,2,3,1,0:T(8,128)}, f32[3,1,16,8,128]{4,2,3,1,0:T(8,128)}, u32[]{:S(2)}, u32[]{:S(2)}) collective-permute-start(f32[3,1,16,8,128]{4,2,3,1,0:T(8,128)} %get-tuple-element.12), channel_id=1, source_target_pairs={{0,16},{16,32},{32,48},{48,64},{64,80},{80,96},{96,112},{112,128},... | collective-permute-start | bytes 589832 | tf_op jit(solution)/shard_map/ppermute | solution.py:15
  237.3 2.2 copy-start.4
  240.5 5.3 %copy-start.2 = (f32[3,8,16,8,128]{4,2,3,1,0:T(8,128)S(1)}, f32[3,8,16,8,128]{4,2,3,1,0:T(8,128)}, u32[]{:S(2)}) copy-start(f32[3,8,16,8,128]{4,2,3,1,0:T(8,128)} %copy-done.1) | copy-start | bytes 4718596
  250.8 233.9 %reduce-scatter.2.cloned.1.call-start = ((), (), s32[]{:S(2)}) async-start(), calls=%async_computation.3 | async-start | bytes 1081344 | tf_op jit(solution)/shard_map/reduce_scatter | solution.py:84
  361.1 16.2 %copy-start.3 = (f32[3,8,16,8,128]{4,2,3,1,0:T(8,128)S(1)}, f32[3,8,16,8,128]{4,2,3,1,0:T(8,128)}, u32[]{:S(2)}) copy-start(f32[3,8,16,8,128]{4,2,3,1,0:T(8,128)} %get-tuple-element.10) | copy-start | bytes 4718596
Sparse Core Ops, SparseCore 0:
  12.0 187.3 all-reduce.3
  250.9 110.1 all-gather.1
  376.7 107.9 reduce-scatter.1
where the time goes:
time: 492 us; the launch traced here: 491 us
  waiting for transfers between devices  403 us (82%)
  other arithmetic  29.3 us (6%)
  matrix products  21 us (4%)
  local copies, waits for them, and re-layouts  19.2 us (4%)
  between operations  13.9 us (3%)
  starting transfers between devices  5.11 us (1%)
    psum x1, waiting for transfers between devices, body(): gram = lax.psum(gram_local, 'space')  187 us
    all_gather x1, waiting for transfers between devices, body(): panel_piece = lax.all_gather(rounded_images, 'mode', axis=4, tiled=True)  110 us
    reduce_scatter x1, waiting for transfers between devices, body(): reduced = lax.psum_scatter(strip, 'space', scatter_dimension=1, tiled=True)  106 us
    dot_general x1, matrix products, body(): jnp.einsum('ra,rk->ak', rounded_rows, piece_rows, preferred_element_type=...  15.4 us
    another operation x3, other arithmetic, body(): lower_factor = jnp.linalg.cholesky(gram)  12.4 us
    another operation x1, other arithmetic, apply_inverse(): jax.scipy.linalg.solve_triangular(lower_factor, flat_rows.T, lower=True)  10.4 us
  transfers between devices with their start and end apart: 5, of which 3 were waited for; matrix products, arithmetic and copies ran while one was open for 3% of the time, Pallas kernels for 0%

commit v1 on v0

--- a/solution.py
+++ b/solution.py
@@ -68,7 +68,7 @@
         )
         * weight
     )
-    gram = lax.psum(gram_local, "space")
+    gram = jnp.sum(lax.all_gather(gram_local, "space"), axis=0)
     lower_factor = jnp.linalg.cholesky(gram)
     ortho = apply_inverse(basis, lower_factor)
     padded_ortho = extended(ortho, (("space", 1),), 1)

time: 492 us -> 374 us (0.76)
  waiting for transfers between devices: 403 us -> 292 us
  matrix products: 21 us -> 15 us
    psum x1 -> x0, waiting for transfers between devices: 187 us -> none  [body(): gram = lax.psum(gram_local, 'space')]
    all_gather x0 -> x1, waiting for transfers between devices: none -> 72.4 us  [body(): gram = jnp.sum(lax.all_gather(gram_local, 'space'), axis=0)]
    dot_general x1, matrix products: 15.4 us -> 9.03 us  [body(): jnp.einsum('ra,rk->ak', rounded_rows, piece_rows, preferred_element_type=...]
  transfers between devices with their start and end apart: 5 -> 5, of which waited for: 3 -> 3; matrix products, arithmetic and copies ran while one was open for 3% -> 4% of each run, Pallas kernels for 0% -> 0%
where the time goes in v1:
time: 374 us
  waiting for transfers between devices  292 us (78%)
  other arithmetic  30.3 us (8%)
  local copies, waits for them, and re-layouts  17.4 us (5%)
  matrix products  15 us (4%)
  between operations  13.9 us (4%)
  starting transfers between devices  5.12 us (1%)
    all_gather x1, waiting for transfers between devices, body(): panel_piece = lax.all_gather(rounded_images, 'mode', axis=4, tiled=True)  112 us
    reduce_scatter x1, waiting for transfers between devices, body(): reduced = lax.psum_scatter(strip, 'space', scatter_dimension=1, tiled=True)  107 us
    all_gather x1, waiting for transfers between devices, body(): gram = jnp.sum(lax.all_gather(gram_local, 'space'), axis=0)  72.4 us
    another operation x3, other arithmetic, body(): lower_factor = jnp.linalg.cholesky(gram)  12.4 us
    another operation x1, other arithmetic, apply_inverse(): jax.scipy.linalg.solve_triangular(lower_factor, flat_rows.T, lower=True)  9.81 us
    dot_general x1, matrix products, body(): jnp.einsum('ra,rk->ak', rounded_rows, piece_rows, preferred_element_type=...  9.03 us
  transfers between devices with their start and end apart: 5, of which 3 were waited for; matrix products, arithmetic and copies ran while one was open for 4% of the time, Pallas kernels for 0%

profile of v1, /device:TPU:2, one launch (start us, length us, event | category | flops | bytes accessed | tf_op | source)
XLA Modules:
  0.0 373.8 jit_solution(15317544143609956054)
XLA Ops:
  7.3 1.3 copy-done
  8.6 3.3 fusion.1
  11.9 0.0 all-gather.4.cloned.1.call-start
  11.9 0.7 copy.45
  12.7 0.7 copy.46
  13.4 0.7 copy.48
  14.1 0.7 copy.47
  14.8 0.1 copy.49
  14.9 0.1 copy.53
  15.0 0.8 copy.51
  15.8 72.4 %all-gather.6.cloned.1.call-done = f32[4096,128]{1,0:T(8,128)} async-done(((f32[128,128]{1,0:T(8,128)}), f32[4096,128]{1,0:T(8,128)}) %all-gather.6.cloned.1.call-update) | async-done | bytes 2097168 | tf_op jit(solution)/shard_map/all_gather | solution.py:71
  88.3 1.7 reduce_sum.9
  90.0 0.1 copy.43
  90.1 11.7 %cholesky.16 = f32[128,128]{1,0:T(8,128)S(1)} custom-call(f32[128,128]{1,0:T(8,128)S(1)} %fusion.4), custom_call_target="Cholesky" | custom-call | tf_op jit(solution)/shard_map/jit(cholesky)/cholesky | solution.py:72
  101.9 0.6 compare_reduce_fusion
  102.5 1.3 fusion.5
  103.8 9.8 %custom-call.7 = f32[1,128,128]{1,2,0:T(8,128)S(1)} custom-call(f32[1,128,128]{2,1,0:T(8,128)S(1)} %get-tuple-element.26), custom_call_target="InvertDiagBlocksLowerTriangular" | custom-call | tf_op jit(solution)/shard_map/jit(_solve_triangular)/triangular_solve | solution.py:51
  113.6 2.7 convolution_bitcast_fusion
  116.3 1.9 copy.44
  118.1 0.8 fusion.7
  118.9 1.3 collective-permute-start
  120.2 3.7 collective-permute-start.1
  123.9 2.6 fusion.8
  126.5 2.0 copy.50
  128.5 2.0 copy.54
  130.5 2.1 copy.52
  132.6 5.1 %fusion.6 = (bf16[3,8,16,8,128]{4,3,2,1,0:T(8,128)(2,1)}, f32[3,8,16,8,128]{4,3,2,1,0:T(8,128)}) fusion(f32[8,16,8,128]{3,2,1,0:T(8,128)} %bitcast.52, f32[3,8,16,8]{3,2,1,0:T(8,128)S(1)} %copy.53, f32[8,16,8,128]{3,2,1,0:T(8,128)} %bitcast.53, f32[3,8,16,8]{3,2,1,0:T(8,128)} %copy.51, f32[8,16,8,128]{3,2,1,0:T(8,128)} %bitcast.51, ...), kind=kLoop, calls=%fused_computation.29 | loop fusion | flops 10616832 | bytes 5951488 | tf_op jit(solution)/shard_map/convert_element_type | solution.py:76
  137.8 0.0 reduce-scatter.2.cloned.1.call-start
  137.8 112.3 %all-gather.4.cloned.1.call-done = bf16[3,8,16,8,2048]{4,3,2,1,0:T(8,128)(2,1)} async-done(((bf16[3,8,16,8,128]{4,3,2,1,0:T(8,128)(2,1)}), bf16[3,8,16,8,2048]{4,3,2,1,0:T(8,128)(2,1)}) %all-gather.4.cloned.1.call-update) | async-done | bytes 12582928 | tf_op jit(solution)/shard_map/all_gather | solution.py:78
  250.2 9.0 %fusion = f32[128,2048]{0,1:T(8,128)} fusion(bf16[3,8,16,8,2048]{4,3,2,1,0:T(8,128)(2,1)} %all-gather.4.cloned.1.call-done, f32[3,8,16,8,128]{4,3,2,1,0:T(8,128)S(1)} %bitcast.50), kind=kOutput, calls=%fused_computation.4 | convolution fusion | flops 1611268096 | bytes 15204352 | tf_op jit(solution)/shard_map/ra,rk->ak/dot_general | solution.py:81
  259.2 0.7 copy.55
  260.0 107.3 %reduce-scatter.2.cloned.1.call-done = f32[128,64]{0,1:T(8,128)} async-done(((f32[128,2048]{0,1:T(8,128)}), f32[128,64]{0,1:T(8,128)}) %reduce-scatter.2.cloned.1.call-update) | async-done | bytes 32784 | tf_op jit(solution)/shard_map/reduce_scatter | solution.py:84
  (19 shorter events, 0.2 us)
Async XLA Ops:
  7.2 1.4 copy-start
  7.2 4.7 %copy-start.4 = (f32[8,16,8]{1,2,0:T(8,128)S(1)}, f32[8,16,8]{1,2,0:T(8,128)}, u32[]{:S(2)}) copy-start(f32[8,16,8]{1,2,0:T(8,128)} %param.7) | copy-start | bytes 12292
  7.2 5.5 %copy-start.3 = (f32[3,8,16,8]{2,3,1,0:T(8,128)S(1)}, f32[3,8,16,8]{2,3,1,0:T(8,128)}, u32[]{:S(2)}) copy-start(f32[3,8,16,8]{2,3,1,0:T(8,128)} %param.5) | copy-start | bytes 36868
  7.2 7.6 %copy-start.1 = (f32[3,3,8,16,8]{3,4,2,1,0:T(8,128)S(1)}, f32[3,3,8,16,8]{3,4,2,1,0:T(8,128)}, u32[]{:S(2)}) copy-start(f32[3,3,8,16,8]{3,4,2,1,0:T(8,128)} %param.6) | copy-start | bytes 110596
  7.2 81.1 %all-gather.6.cloned.1.call-start = ((), (), s32[]{:S(2)}) async-start(), calls=%async_computation.3 | async-start | bytes 2162688 | tf_op jit(solution)/shard_map/all_gather | solution.py:71
  11.9 238.3 %all-gather.4.cloned.1.call-start = ((), (), s32[]{:S(2)}) async-start(), calls=%async_computation.1 | async-start | bytes 13369344 | tf_op jit(solution)/shard_map/all_gather | solution.py:78
  118.9 13.7 %collective-permute-start = (f32[3,1,16,8,128]{4,3,2,1,0:T(8,128)}, f32[3,1,16,8,128]{4,3,2,1,0:T(8,128)}, u32[]{:S(2)}, u32[]{:S(2)}) collective-permute-start(f32[3,1,16,8,128]{4,3,2,1,0:T(8,128)} %get-tuple-element.14), channel_id=1, source_target_pairs={{16,0},{32,16},{48,32},{64,48},{80,64},{96,80},{112,96},{128,112},... | collective-permute-start | bytes 589832 | tf_op jit(solution)/shard_map/ppermute | solution.py:17
  120.2 12.4 %collective-permute-start.1 = (f32[3,1,16,8,128]{4,3,2,1,0:T(8,128)}, f32[3,1,16,8,128]{4,3,2,1,0:T(8,128)}, u32[]{:S(2)}, u32[]{:S(2)}) collective-permute-start(f32[3,1,16,8,128]{4,3,2,1,0:T(8,128)} %get-tuple-element.15), channel_id=1, source_target_pairs={{0,16},{16,32},{32,48},{48,64},{64,80},{80,96},{96,112},{112,128},... | collective-permute-start | bytes 589832 | tf_op jit(solution)/shard_map/ppermute | solution.py:15
  137.8 121.5 %copy-start.2 = (f32[128,128]{0,1:T(8,128)S(1)}, f32[128,128]{0,1:T(8,128)}, u32[]{:S(2)}) copy-start(f32[128,128]{0,1:T(8,128)} %get-tuple-element.25) | copy-start | bytes 196612
  137.8 229.5 %reduce-scatter.2.cloned.1.call-start = ((), (), s32[]{:S(2)}) async-start(), calls=%async_computation.2 | async-start | bytes 1081344 | tf_op jit(solution)/shard_map/reduce_scatter | solution.py:84
Sparse Core Ops, SparseCore 0:
  12.0 76.2 all-gather.5
  137.9 112.2 all-gather.3
  259.3 107.9 reduce-scatter.1
